TPU v7x, 32 devices: a whole 2x2x4 slice. The times are simulated.
32 devices in a mesh: egrp: 4 (over y, x), inner: 8 (over z, core).
Axes of the slice: x: 2, y: 2, z: 4, core: 2. Of those that a mesh axis runs over, the one named last changes fastest.
Arguments:
- retarded: float32 [32, 2, 16, 128, 128], P(('egrp', 'inner')), may hold values from -0.31819806 to 0.31819806
- injection: float32 [32, 2, 16, 128, 128], P(('egrp', 'inner')), may hold values from -6 to 6
- coupling_matrices: float32 [2, 128, 128], replicated, may hold values from -0.5 to 0.5
- phonon_weight: float32 [2, 2], replicated, may hold values from 0.3 to 1
- phonon_shift: int32 [2], replicated, may hold values from 1 to 8, as said below
- slice_neighbour: int32 [16], replicated, may hold values from 0 to 15, as said below
Outputs:
- lesser_green: float32 [32, 2, 16, 128, 128], P(('egrp', 'inner'))
- phonon_sigma: float32 [32, 2, 16, 128, 128], P(('egrp', 'inner'))
Inputs may be any that keep to these rules, and one draw needn't show every extreme that they name: `phonon_shift`: every entry is at least 1, and one entry equals 8. `slice_neighbour`: entry s is s - 1 or s + 1.
All inputs are finite; a program needn't handle non-finite values.
Results may differ from a plain program's by a relative error of at most 0.00015.
Values sent between devices are 32-bit elements; how exact they have to be, the bound alone decides.
A program may use at most 64 MiB of HBM per device.

v0:
```python
import jax
import jax.numpy as jnp
from jax import lax
from jax.sharding import PartitionSpec as P

MAXSHIFT = 8
ITERS = 2


HIGHEST = lax.Precision.HIGHEST


def padded(block, sides, width):
    for axis, dim in sides:
        count = lax.axis_size(axis)
        forward = [(i, i + 1) for i in range(count - 1)]
        backward = [(target, source) for source, target in forward]
        low = lax.ppermute(
            lax.slice_in_dim(block, block.shape[dim] - width, None, axis=dim), axis, forward
        )
        high = lax.ppermute(lax.slice_in_dim(block, 0, width, axis=dim), axis, backward)
        block = jnp.concatenate([low, block, high], axis=dim)
    return block


def product(first, second):
    return jnp.einsum("...ij,...jk->...ik", first, second, precision=HIGHEST)


def product_adjoint(first, second):
    return jnp.einsum("...ij,...kj->...ik", first, second, precision=HIGHEST)


def sandwich(green_ret, source):
    real_green, imag_green = (green_ret[:, 0], green_ret[:, 1])
    real_source, imag_source = (source[:, 0], source[:, 1])
    real_inner = product(real_green, real_source) - product(imag_green, imag_source)
    imag_inner = product(real_green, imag_source) + product(imag_green, real_source)
    real_outer = product_adjoint(real_inner, real_green) + product_adjoint(imag_inner, imag_green)
    imag_outer = product_adjoint(imag_inner, real_green) - product_adjoint(real_inner, imag_green)
    return jnp.stack([real_outer, imag_outer], axis=1)


def project(matrix, blocks):
    halfway = jnp.einsum("ij,...jk->...ik", matrix, blocks, precision=HIGHEST)
    return jnp.einsum("...ik,lk->...il", halfway, matrix, precision=HIGHEST)


def pick_slices(onehot, blocks):
    return jnp.einsum("st,ectij->ecsij", onehot, blocks, precision=HIGHEST)


def couple_block(owned, coupling_matrices, phonon_weight, phonon_shift):
    extended = padded(owned, (("egrp", 0),), MAXSHIFT)
    energies = owned.shape[0]
    accumulated = jnp.zeros(owned.shape, jnp.float32)
    for phonon in range(coupling_matrices.shape[0]):
        shifted_up = lax.dynamic_slice_in_dim(
            extended, MAXSHIFT + phonon_shift[phonon], energies, 0
        )
        shifted_down = lax.dynamic_slice_in_dim(
            extended, MAXSHIFT - phonon_shift[phonon], energies, 0
        )
        summed = phonon_weight[phonon, 0] * shifted_up + phonon_weight[phonon, 1] * shifted_down
        accumulated = accumulated + project(coupling_matrices[phonon], summed)
    return accumulated


def local(retarded, injection, coupling_matrices, phonon_weight, phonon_shift, slice_neighbour):
    groups = lax.axis_size("inner")
    all_slices = slice_neighbour.shape[0]
    green_owned, inject_owned = (
        lax.all_to_all(retarded, "inner", split_axis=2, concat_axis=0, tiled=True),
        lax.all_to_all(injection, "inner", split_axis=2, concat_axis=0, tiled=True),
    )
    local_count = all_slices // groups
    base = lax.axis_index("inner") * local_count
    neighbours = lax.dynamic_slice_in_dim(slice_neighbour, base, local_count, 0)
    position = neighbours - base + 1
    onehot = (position[:, None] == jnp.arange(local_count + 2)[None, :]).astype(jnp.float32)
    phonon_sigma = jnp.zeros_like(green_owned)
    lesser = jnp.zeros_like(green_owned)
    for iteration in range(ITERS):
        lesser = sandwich(green_owned, inject_owned + phonon_sigma)
        rims = padded(lesser, (("inner", 2),), 1)
        mixed_green = lesser + 0.5 * pick_slices(onehot, rims)
        phonon_sigma = couple_block(mixed_green, coupling_matrices, phonon_weight, phonon_shift)
    lesser_out, sigma_out = (
        lax.all_to_all(lesser, "inner", split_axis=0, concat_axis=2, tiled=True),
        lax.all_to_all(phonon_sigma, "inner", split_axis=0, concat_axis=2, tiled=True),
    )
    return (lesser_out, sigma_out)


def solution(mesh):
    placed = (
        P(("egrp", "inner"), None, None, None, None),
        P(("egrp", "inner"), None, None, None, None),
        P(),
        P(),
        P(),
        P(),
    )
    return jax.shard_map(
        local,
        mesh=mesh,
        in_specs=placed,
        out_specs=(
            P(("egrp", "inner"), None, None, None, None),
            P(("egrp", "inner"), None, None, None, None),
        ),
        check_vma=False,
    )
```

profile of v0, /device:TPU:0, one launch (start us, length us, event | category | flops | bytes accessed | tf_op | source)
XLA Modules:
  0.0 488.0 jit_solution(7137571596730429825)
XLA Ops:
  3.8 6.3 %all-to-all-start.1 = ((f32[1,2,16,128,128]{4,3,1,0,2:T(8,128)}), f32[1,2,16,128,128]{4,3,1,0,2:T(8,128)S(1)}, u32[]{:S(2)}, u32[]{:S(2)}) async-start(f32[1,2,16,128,128]{4,3,1,0,2:T(8,128)} %copy.67), calls=%async_computation.1 | async-start | bytes 4194304 | tf_op jit(solution)/shard_map/all_to_all | solution.py:73
  13.2 45.9 %all-to-all-done.1 = f32[1,2,16,128,128]{4,3,1,0,2:T(8,128)S(1)} async-done(((f32[1,2,16,128,128]{4,3,1,0,2:T(8,128)}), f32[1,2,16,128,128]{4,3,1,0,2:T(8,128)S(1)}, u32[]{:S(2)}, u32[]{:S(2)}) %all-to-all-start.1) | async-done | bytes 2097184 | tf_op jit(solution)/shard_map/all_to_all | solution.py:73
  60.5 4.4 all-to-all-start
  66.6 47.3 %all-to-all-done = f32[1,2,16,128,128]{4,3,1,0,2:T(8,128)} async-done(((f32[1,2,16,128,128]{4,3,1,0,2:T(8,128)}), f32[1,2,16,128,128]{4,3,1,0,2:T(8,128)}, u32[]{:S(2)}, u32[]{:S(2)}) %all-to-all-start) | async-done | bytes 2097184 | tf_op jit(solution)/shard_map/all_to_all | solution.py:74
  140.9 5.3 %fusion.2 = f32[8,2,128,128,2]{3,4,2,1,0:T(2,128)S(1)} fusion(f32[8,2,4,128,128]{4,3,2,0,1:T(8,128)S(1)} %pad_maximum_fusion.2, s32[2]{0:T(128)S(1)} %subtract_add_fusion), kind=kOutput, calls=%fused_computation.6 | convolution fusion | flops 25165832 | bytes 6291464 | tf_op jit(solution)/shard_map/st,ectij->ecsij/dot_general | solution.py:50
  147.9 4.7 collective-permute-start.2
  160.3 27.6 %collective-permute-done.2 = f32[8,2,2,128,128]{4,3,2,0,1:T(8,128)} collective-permute-done((f32[8,2,2,128,128]{4,3,2,0,1:T(8,128)}, f32[8,2,2,128,128]{4,3,2,0,1:T(8,128)}, u32[]{:S(2)}, u32[]{:S(2)}) %collective-permute-start.2) | collective-permute-done | bytes 2097184 | tf_op jit(solution)/shard_map/ppermute | solution.py:18
  187.9 46.9 %collective-permute-done.3 = f32[8,2,2,128,128]{4,3,2,0,1:T(8,128)} collective-permute-done((f32[8,2,2,128,128]{4,3,2,0,1:T(8,128)}, f32[8,2,2,128,128]{4,3,2,0,1:T(8,128)}, u32[]{:S(2)}, u32[]{:S(2)}) %collective-permute-start.3) | collective-permute-done | bytes 2097184 | tf_op jit(solution)/shard_map/ppermute | solution.py:21
  238.1 3.7 multiply_add_fusion.3
  241.9 3.5 fusion.24
  245.4 3.5 fusion.13
  252.4 3.6 add_add_fusion
  271.9 11.5 %collective-permute-start.4 = (f32[8,2,1,128,128]{4,3,2,0,1:T(8,128)S(1)}, f32[8,2,1,128,128]{4,3,2,0,1:T(8,128)S(1)}, u32[]{:S(2)}, u32[]{:S(2)}) collective-permute-start(f32[8,2,1,128,128]{4,3,2,0,1:T(8,128)S(1)} %get-tuple-element.8), channel_id=1, source_target_pairs={{0,1},{1,2},{2,3},{3,4},{4,5},{5,6},{6,7},{8,9},{9,10},{10,11},{11... | collective-permute-start | bytes 3145736 | tf_op jit(solution)/shard_map/ppermute | solution.py:18
  285.6 12.3 %collective-permute-done.5 = f32[8,2,1,128,128]{4,3,2,0,1:T(8,128)S(1)} collective-permute-done((f32[8,2,1,128,128]{4,3,2,0,1:T(8,128)S(1)}, f32[8,2,1,128,128]{4,3,2,0,1:T(8,128)S(1)}, u32[]{:S(2)}, u32[]{:S(2)}) %collective-permute-start.5) | collective-permute-done | bytes 1048608 | tf_op jit(solution)/shard_map/ppermute | solution.py:21
  298.2 5.3 %fusion = f32[8,2,128,128,2]{3,4,2,1,0:T(2,128)S(1)} fusion(f32[8,2,4,128,128]{4,3,2,0,1:T(8,128)S(1)} %pad_maximum_fusion.3, s32[2]{0:T(128)S(1)} %subtract_add_fusion), kind=kOutput, calls=%fused_computation.4 | convolution fusion | flops 25165832 | bytes 6291464 | tf_op jit(solution)/shard_map/st,ectij->ecsij/dot_general | solution.py:50
  305.3 4.7 collective-permute-start.6
  312.8 13.4 %all-to-all-start.2 = ((f32[8,2,2,128,128]{4,3,2,1,0:T(8,128)}), f32[8,2,2,128,128]{4,3,2,1,0:T(8,128)S(1)}, u32[]{:S(2)}, u32[]{:S(2)}) async-start(f32[8,2,2,128,128]{4,3,2,1,0:T(8,128)} %copy.85), calls=%async_computation.2 | async-start | bytes 4194304 | tf_op jit(solution)/shard_map/all_to_all | solution.py:89
  326.2 17.6 %collective-permute-done.6 = f32[8,2,2,128,128]{4,3,2,0,1:T(8,128)} collective-permute-done((f32[8,2,2,128,128]{4,3,2,0,1:T(8,128)}, f32[8,2,2,128,128]{4,3,2,0,1:T(8,128)}, u32[]{:S(2)}, u32[]{:S(2)}) %collective-permute-start.6) | collective-permute-done | bytes 2097184 | tf_op jit(solution)/shard_map/ppermute | solution.py:18
  343.9 45.1 %collective-permute-done.7 = f32[8,2,2,128,128]{4,3,2,0,1:T(8,128)} collective-permute-done((f32[8,2,2,128,128]{4,3,2,0,1:T(8,128)}, f32[8,2,2,128,128]{4,3,2,0,1:T(8,128)}, u32[]{:S(2)}, u32[]{:S(2)}) %collective-permute-start.7) | collective-permute-done | bytes 2097184 | tf_op jit(solution)/shard_map/ppermute | solution.py:21
  392.3 3.7 multiply_add_fusion.1
  396.0 3.5 fusion.7
  406.5 5.1 %fusion.29 = f32[8,2,2,128,128]{4,3,2,1,0:T(8,128)} fusion(f32[8,2,2,128,128]{4,3,2,1,0:T(8,128)S(1)} %fusion.5, f32[8,2,2,128,128]{4,3,2,1,0:T(8,128)S(1)} %fusion.11, f32[2,128,128]{2,1,0:T(8,128)S(1)} %copy-done.5), kind=kOutput, calls=%fused_computation.45 | convolution fusion | flops 805830656 | bytes 6356992 | tf_op jit(solution)/shard_map/...ik,lk->...il/dot_general | solution.py:46
  411.6 24.0 %all-to-all-start.3 = ((f32[8,2,2,128,128]{4,3,2,1,0:T(8,128)}), f32[8,2,2,128,128]{4,3,2,1,0:T(8,128)}, u32[]{:S(2)}, u32[]{:S(2)}) async-start(f32[8,2,2,128,128]{4,3,2,1,0:T(8,128)} %fusion.29), calls=%async_computation.3 | async-start | bytes 4194304 | tf_op jit(solution)/shard_map/all_to_all | solution.py:90
  437.0 47.7 %all-to-all-done.3 = f32[8,2,2,128,128]{4,3,2,1,0:T(8,128)} async-done(((f32[8,2,2,128,128]{4,3,2,1,0:T(8,128)}), f32[8,2,2,128,128]{4,3,2,1,0:T(8,128)}, u32[]{:S(2)}, u32[]{:S(2)}) %all-to-all-start.3) | async-done | bytes 2097184 | tf_op jit(solution)/shard_map/all_to_all | solution.py:90
  (64 shorter events, 84.9 us)
Async XLA Ops:
  3.8 55.4 %all-to-all-start.1 = ((f32[1,2,16,128,128]{4,3,1,0,2:T(8,128)}), f32[1,2,16,128,128]{4,3,1,0,2:T(8,128)S(1)}, u32[]{:S(2)}, u32[]{:S(2)}) async-start(f32[1,2,16,128,128]{4,3,1,0,2:T(8,128)} %copy.67), calls=%async_computation.1 | async-start | bytes 4194304 | tf_op jit(solution)/shard_map/all_to_all | solution.py:73
  59.2 1.3 copy-start.4
  60.5 53.4 %all-to-all-start = ((f32[1,2,16,128,128]{4,3,1,0,2:T(8,128)}), f32[1,2,16,128,128]{4,3,1,0,2:T(8,128)}, u32[]{:S(2)}, u32[]{:S(2)}) async-start(f32[1,2,16,128,128]{4,3,1,0,2:T(8,128)} %copy.65), calls=%async_computation | async-start | bytes 4194304 | tf_op jit(solution)/shard_map/all_to_all | solution.py:74
  115.6 5.9 %copy-start = (f32[1,2,16,128,128]{4,3,2,1,0:T(8,128)}, f32[1,2,16,128,128]{4,3,2,1,0:T(8,128)S(1)}, u32[]{:S(2)}) copy-start(f32[1,2,16,128,128]{4,3,2,1,0:T(8,128)S(1)} %copy.66) | copy-start | bytes 6291460
  129.7 1.7 copy-start.2
  129.7 5.9 %copy-start.8 = (s32[16]{0:T(128)S(1)}, s32[16]{0:T(128)}, u32[]{:S(2)}) copy-start(s32[16]{0:T(128)} %param.11) | copy-start | bytes 196
  131.3 4.3 collective-permute-start
  133.8 4.9 %collective-permute-start.1 = (f32[8,2,1,128,128]{4,3,2,0,1:T(8,128)}, f32[8,2,1,128,128]{4,3,2,0,1:T(8,128)}, u32[]{:S(2)}, u32[]{:S(2)}) collective-permute-start(f32[8,2,1,128,128]{4,3,2,0,1:T(8,128)} %get-tuple-element.11), channel_id=1, source_target_pairs={{1,0},{2,1},{3,2},{4,3},{5,4},{6,5},{7,6},{9,8},{10,9},{11,10},{12... | collective-permute-start | bytes 3145736 | tf_op jit(solution)/shard_map/ppermute | solution.py:21
  140.9 5.3 %copy-start.3 = (f32[8,1,2,128,128]{4,3,2,0,1:T(8,128)S(1)}, f32[8,1,2,128,128]{4,3,2,0,1:T(8,128)}, u32[]{:S(2)}) copy-start(f32[8,1,2,128,128]{4,3,2,0,1:T(8,128)} %copy-done.2) | copy-start | bytes 3145732
  146.2 7.7 %copy-start.7 = (s32[2]{0:T(128)S(1)}, s32[2]{0:T(128)}, u32[]{:S(2)}) copy-start(s32[2]{0:T(128)} %param.10) | copy-start | bytes 28
  146.2 13.4 %copy-start.6 = (f32[2,2]{1,0:T(2,128)S(1)}, f32[2,2]{1,0:T(2,128)}, u32[]{:S(2)}) copy-start(f32[2,2]{1,0:T(2,128)} %param.9) | copy-start | bytes 52
  147.9 40.0 %collective-permute-start.2 = (f32[8,2,2,128,128]{4,3,2,0,1:T(8,128)}, f32[8,2,2,128,128]{4,3,2,0,1:T(8,128)}, u32[]{:S(2)}, u32[]{:S(2)}) collective-permute-start(f32[8,2,2,128,128]{4,3,2,0,1:T(8,128)} %fusion.4), channel_id=1, source_target_pairs={{0,8},{8,16},{16,24},{1,9},{9,17},{17,25},{2,10},{10,18},{18,26},{... | collective-permute-start | bytes 6291464 | tf_op jit(solution)/shard_map/ppermute | solution.py:18
  152.6 82.2 %collective-permute-start.3 = (f32[8,2,2,128,128]{4,3,2,0,1:T(8,128)}, f32[8,2,2,128,128]{4,3,2,0,1:T(8,128)}, u32[]{:S(2)}, u32[]{:S(2)}) collective-permute-start(f32[8,2,2,128,128]{4,3,2,0,1:T(8,128)} %fusion.4), channel_id=1, source_target_pairs={{8,0},{16,8},{24,16},{9,1},{17,9},{25,17},{10,2},{18,10},{26,18},{... | collective-permute-start | bytes 6291464 | tf_op jit(solution)/shard_map/ppermute | solution.py:21
  238.1 3.8 copy-start.5
  248.9 3.5 copy-start.1
  271.9 13.7 %collective-permute-start.4 = (f32[8,2,1,128,128]{4,3,2,0,1:T(8,128)S(1)}, f32[8,2,1,128,128]{4,3,2,0,1:T(8,128)S(1)}, u32[]{:S(2)}, u32[]{:S(2)}) collective-permute-start(f32[8,2,1,128,128]{4,3,2,0,1:T(8,128)S(1)} %get-tuple-element.8), channel_id=1, source_target_pairs={{0,1},{1,2},{2,3},{3,4},{4,5},{5,6},{6,7},{8,9},{9,10},{10,11},{11... | collective-permute-start | bytes 3145736 | tf_op jit(solution)/shard_map/ppermute | solution.py:18
  283.4 14.5 %collective-permute-start.5 = (f32[8,2,1,128,128]{4,3,2,0,1:T(8,128)S(1)}, f32[8,2,1,128,128]{4,3,2,0,1:T(8,128)S(1)}, u32[]{:S(2)}, u32[]{:S(2)}) collective-permute-start(f32[8,2,1,128,128]{4,3,2,0,1:T(8,128)S(1)} %get-tuple-element.9), channel_id=1, source_target_pairs={{1,0},{2,1},{3,2},{4,3},{5,4},{6,5},{7,6},{9,8},{10,9},{11,10},{12... | collective-permute-start | bytes 3145736 | tf_op jit(solution)/shard_map/ppermute | solution.py:21
  305.3 38.6 %collective-permute-start.6 = (f32[8,2,2,128,128]{4,3,2,0,1:T(8,128)}, f32[8,2,2,128,128]{4,3,2,0,1:T(8,128)}, u32[]{:S(2)}, u32[]{:S(2)}) collective-permute-start(f32[8,2,2,128,128]{4,3,2,0,1:T(8,128)} %get-tuple-element.6), channel_id=1, source_target_pairs={{0,8},{8,16},{16,24},{1,9},{9,17},{17,25},{2,10},{10,18},{18,26},{... | collective-permute-start | bytes 6291464 | tf_op jit(solution)/shard_map/ppermute | solution.py:18
  310.0 79.0 %collective-permute-start.7 = (f32[8,2,2,128,128]{4,3,2,0,1:T(8,128)}, f32[8,2,2,128,128]{4,3,2,0,1:T(8,128)}, u32[]{:S(2)}, u32[]{:S(2)}) collective-permute-start(f32[8,2,2,128,128]{4,3,2,0,1:T(8,128)} %get-tuple-element.6), channel_id=1, source_target_pairs={{8,0},{16,8},{24,16},{9,1},{17,9},{25,17},{10,2},{18,10},{26,18},{... | collective-permute-start | bytes 6291464 | tf_op jit(solution)/shard_map/ppermute | solution.py:21
  312.8 98.8 %all-to-all-start.2 = ((f32[8,2,2,128,128]{4,3,2,1,0:T(8,128)}), f32[8,2,2,128,128]{4,3,2,1,0:T(8,128)S(1)}, u32[]{:S(2)}, u32[]{:S(2)}) async-start(f32[8,2,2,128,128]{4,3,2,1,0:T(8,128)} %copy.85), calls=%async_computation.2 | async-start | bytes 4194304 | tf_op jit(solution)/shard_map/all_to_all | solution.py:89
  411.6 73.1 %all-to-all-start.3 = ((f32[8,2,2,128,128]{4,3,2,1,0:T(8,128)}), f32[8,2,2,128,128]{4,3,2,1,0:T(8,128)}, u32[]{:S(2)}, u32[]{:S(2)}) async-start(f32[8,2,2,128,128]{4,3,2,1,0:T(8,128)} %fusion.29), calls=%async_computation.3 | async-start | bytes 4194304 | tf_op jit(solution)/shard_map/all_to_all | solution.py:90
where the time goes:
time: 497 us; the launch traced here: 488 us
  waiting for transfers between devices  295 us (59%)
  starting transfers between devices  77.1 us (16%)
  matrix products  69.8 us (14%)
  other arithmetic  21.9 us (4%)
  local copies, waits for them, and re-layouts  18.5 us (4%)
  between operations  6.26 us (1%)
    ppermute x4, waiting for transfers between devices, padded(): lax.ppermute(lax.slice_in_dim(block, 0, width, axis=dim), axis, backward)  107 us
    all_to_all x1, waiting for transfers between devices, local(): lax.all_to_all(phonon_sigma, 'inner', split_axis=0, concat_axis=2, tiled=...  47.7 us
    all_to_all x1, waiting for transfers between devices, local(): lax.all_to_all(injection, 'inner', split_axis=2, concat_axis=0, tiled=True)  47.3 us
    ppermute x4, waiting for transfers between devices, padded(): lax.ppermute(lax.slice_in_dim(block, block.shape[dim] - width, None, axis...  46.2 us
    all_to_all x1, waiting for transfers between devices, local(): lax.all_to_all(retarded, 'inner', split_axis=2, concat_axis=0, tiled=True)  45.9 us
    all_to_all x1, starting transfers between devices, local(): lax.all_to_all(phonon_sigma, 'inner', split_axis=0, concat_axis=2, tiled=...  24 us
    ppermute x4, starting transfers between devices, padded(): lax.ppermute(lax.slice_in_dim(block, block.shape[dim] - width, None, axis...  23.4 us
    dot_general x8, matrix products, product_adjoint(): return jnp.einsum('...ij,...kj->...ik', first, second, precision=HIGHEST)  17 us
  transfers between devices with their start and end apart: 12, of which 10 were waited for; matrix products, arithmetic and copies ran while one was open for 6% of the time, Pallas kernels for 0%

commit v1 on v0

v1 whole, which is shorter than its diff:
```python
import functools

import jax
import jax.numpy as jnp
from jax import lax
from jax.experimental import pallas as pl
from jax.experimental.pallas import tpu as pltpu
from jax.sharding import PartitionSpec as P

MAXSHIFT = 8
ITERS = 2

MESH = pl.DeviceIdType.MESH
F32 = jnp.float32
BF16 = jnp.bfloat16


def halves(x):
    high = x.astype(BF16)
    return high, (x - high.astype(F32)).astype(BF16)


def dot3(first, second, dims):
    (first_high, first_low), (second_high, second_low) = first, second

    def one(a, b):
        return lax.dot_general(a, b, (dims, ((), ())), preferred_element_type=F32)

    return one(first_high, second_high) + (
        one(first_high, second_low) + one(first_low, second_high)
    )


PLAIN = ((1,), (0,))
ADJOINT = ((1,), (1,))


def kernel(
    groups, inner, pairs,
    ret_ref, inj_ref, coupling_ref, weight_ref, shift_ref, near_ref,
    lesser_ref, sigma_ref,
    mix_buf, k_buf, sig_buf,
    mix_send, mix_recv, sig_send, sig_recv, halo_send, halo_recv,
    *x_bufs,
):
    me = lax.axis_index("egrp") * inner + lax.axis_index("inner")
    group, mine = me // pairs, me % pairs
    my_slice, my_part = mine // 2, mine % 2
    slices = pairs // 2

    def device(flat):
        return (flat // inner, flat % inner)

    barrier = pltpu.get_barrier_semaphore()

    def greet(step, carry):
        other = group * pairs + (mine + step) % pairs
        pl.semaphore_signal(barrier, inc=1, device_id=device(other), device_id_type=MESH)
        return carry

    lax.fori_loop(1, pairs, greet, 0)
    if groups > 1:
        for side in (-1, 1):
            @pl.when((group + side >= 0) & (group + side < groups))
            def _():
                def greet_side(step, carry):
                    other = (group + side) * pairs + step
                    pl.semaphore_signal(
                        barrier, inc=1, device_id=device(other), device_id_type=MESH
                    )
                    return carry

                lax.fori_loop(0, pairs, greet_side, 0)

    zeros = jnp.zeros((MAXSHIFT,) + x_bufs[0].shape[1:], F32)
    for iteration in range(ITERS):
        @pl.when(group == 0)
        def _():
            x_bufs[iteration][pl.ds(0, MAXSHIFT)] = zeros

        @pl.when(group == groups - 1)
        def _():
            x_bufs[iteration][pl.ds(MAXSHIFT + pairs, MAXSHIFT)] = zeros

    def sandwich(iteration, s):
        source_real, source_imag = inj_ref[0, s], inj_ref[1, s]
        if iteration > 0:
            source_real = source_real + sig_buf[0, s]
            source_imag = source_imag + sig_buf[1, s]
        green_real, green_imag = halves(ret_ref[0, s]), halves(ret_ref[1, s])
        source_real, source_imag = halves(source_real), halves(source_imag)
        left = [jnp.concatenate([r, i], axis=1) for r, i in zip(green_real, green_imag)]
        middle = [
            jnp.concatenate(
                [jnp.concatenate([r, i], axis=1), jnp.concatenate([-i, r], axis=1)], axis=0
            )
            for r, i in zip(source_real, source_imag)
        ]
        right = [
            jnp.concatenate(
                [jnp.concatenate([r, i], axis=1), jnp.concatenate([-i, r], axis=1)], axis=0
            )
            for r, i in zip(green_real, green_imag)
        ]
        held = halves(dot3(left, middle, PLAIN))
        outer = dot3(held, right, ADJOINT)
        width = outer.shape[1] // 2
        lesser_ref[0, s] = outer[:, :width]
        lesser_ref[1, s] = outer[:, width:]

    def mix_copy(iteration, pair, owner):
        return pltpu.make_async_remote_copy(
            src_ref=mix_buf.at[iteration, pair],
            dst_ref=x_bufs[iteration].at[MAXSHIFT + owner],
            send_sem=mix_send.at[iteration, pair],
            recv_sem=mix_recv.at[iteration, owner],
            device_id=device(group * pairs + pair),
            device_id_type=MESH,
        )

    def halo_copy(iteration, side, pair):
        slot = mine % MAXSHIFT
        there = (MAXSHIFT + pairs if side == 0 else 0) + slot
        return pltpu.make_async_remote_copy(
            src_ref=mix_buf.at[iteration, pair],
            dst_ref=x_bufs[iteration].at[there],
            send_sem=halo_send.at[iteration, side, pair],
            recv_sem=halo_recv.at[iteration, side, slot],
            device_id=device((group + (1 if side else -1)) * pairs + pair),
            device_id_type=MESH,
        )

    def halo_arrival(iteration, side, slot):
        there = (MAXSHIFT + pairs if side == 0 else 0) + slot
        return pltpu.make_async_remote_copy(
            src_ref=mix_buf.at[iteration, 0],
            dst_ref=x_bufs[iteration].at[there],
            send_sem=halo_send.at[iteration, side, 0],
            recv_sem=halo_recv.at[iteration, side, slot],
            device_id=device(me),
            device_id_type=MESH,
        )

    def sends_halo(side):
        if side == 0:
            return (group > 0) & (mine < MAXSHIFT)
        return (group < groups - 1) & (mine >= pairs - MAXSHIFT)

    def gets_halo(side):
        return group < groups - 1 if side == 0 else group > 0

    def sigma_copy(iteration, energy, pair):
        target = sig_buf if iteration + 1 < ITERS else sigma_ref
        return pltpu.make_async_remote_copy(
            src_ref=k_buf.at[iteration, energy],
            dst_ref=target.at[pair % 2, pair // 2],
            send_sem=sig_send.at[iteration, energy],
            recv_sem=sig_recv.at[iteration, pair],
            device_id=device(group * pairs + energy),
            device_id_type=MESH,
        )

    coupling = [halves(coupling_ref[m]) for m in range(coupling_ref.shape[0])]
    wide = [jnp.concatenate(list(part), axis=1) for part in zip(*coupling)]

    def couple(iteration, energy):
        halfway = []
        for m in range(len(coupling)):
            shift = shift_ref[m]
            summed = (
                weight_ref[m, 0] * x_bufs[iteration][MAXSHIFT + energy + shift]
                + weight_ref[m, 1] * x_bufs[iteration][MAXSHIFT + energy - shift]
            )
            halfway.append(halves(dot3(coupling[m], halves(summed), PLAIN)))
        joined = [jnp.concatenate(list(part), axis=1) for part in zip(*halfway)]
        return dot3(joined, wide, ADJOINT)

    for iteration in range(ITERS):
        def do_sandwich(s, carry):
            sandwich(iteration, s)
            return carry

        lax.fori_loop(0, slices, do_sandwich, 0)

        if iteration == 0:
            if groups > 1:
                sides = (group > 0).astype(jnp.int32) + (group < groups - 1).astype(jnp.int32)
                pl.semaphore_wait(barrier, pairs - 1 + sides * pairs)
            else:
                pl.semaphore_wait(barrier, pairs - 1)

        def mixed(pair):
            part, s = pair % 2, pair // 2
            return lesser_ref[part, s] + 0.5 * lesser_ref[part, near_ref[s]]

        def do_mix(step, carry):
            pair = (mine + step) % pairs
            mix_buf[iteration, pair] = mixed(pair)
            mix_copy(iteration, pair, mine).start()
            if groups > 1:
                for side in (0, 1):
                    @pl.when(sends_halo(side))
                    def _():
                        halo_copy(iteration, side, pair).start()
            return carry

        lax.fori_loop(1, pairs, do_mix, 0)
        own = mixed(mine)
        x_bufs[iteration][MAXSHIFT + mine] = own
        if groups > 1:
            mix_buf[iteration, mine] = own
            for side in (0, 1):
                @pl.when(sends_halo(side))
                def _():
                    halo_copy(iteration, side, mine).start()

        def mix_arrives(step, carry):
            mix_copy(iteration, mine, (mine + pairs - step) % pairs).wait_recv()
            return carry

        lax.fori_loop(1, pairs, mix_arrives, 0)
        if groups > 1:
            for side in (0, 1):
                @pl.when(gets_halo(side))
                def _():
                    for slot in range(MAXSHIFT):
                        halo_arrival(iteration, side, slot).wait_recv()

        def do_couple(step, carry):
            energy = (mine + step) % pairs
            k_buf[iteration, energy] = couple(iteration, energy)
            sigma_copy(iteration, energy, mine).start()
            return carry

        lax.fori_loop(1, pairs, do_couple, 0)
        target = sig_buf if iteration + 1 < ITERS else sigma_ref
        target[my_part, my_slice] = couple(iteration, mine)

        def sigma_arrives(step, carry):
            sigma_copy(iteration, mine, (mine + pairs - step) % pairs).wait_recv()
            return carry

        lax.fori_loop(1, pairs, sigma_arrives, 0)

    def drain(step, carry):
        other = (mine + step) % pairs
        for iteration in range(ITERS):
            mix_copy(iteration, other, mine).wait_send()
            sigma_copy(iteration, other, mine).wait_send()
        return carry

    lax.fori_loop(1, pairs, drain, 0)
    if groups > 1:
        for side in (0, 1):
            @pl.when(sends_halo(side))
            def _():
                def drain_side(pair, carry):
                    for iteration in range(ITERS):
                        halo_copy(iteration, side, pair).wait_send()
                    return carry

                lax.fori_loop(0, pairs, drain_side, 0)


def local(groups, inner, retarded, injection, coupling_matrices, phonon_weight, phonon_shift, slice_neighbour):
    shape = retarded.shape[1:]
    block = shape[2:]
    pairs = shape[0] * shape[1]
    vmem = pl.BlockSpec(memory_space=pltpu.VMEM)
    smem = pl.BlockSpec(memory_space=pltpu.SMEM)
    sems = pltpu.SemaphoreType.DMA
    flops = ITERS * pairs * 8 * 3 * 2 * block[0] ** 3
    lesser, sigma = pl.pallas_call(
        functools.partial(kernel, groups, inner, pairs),
        out_shape=[jax.ShapeDtypeStruct(shape, F32)] * 2,
        in_specs=[vmem, vmem, vmem, smem, smem, smem],
        out_specs=[vmem, vmem],
        scratch_shapes=[
            pltpu.VMEM((ITERS, pairs) + block, F32),
            pltpu.VMEM((ITERS, pairs) + block, F32),
            pltpu.VMEM(shape, F32),
            sems((ITERS, pairs)),
            sems((ITERS, pairs)),
            sems((ITERS, pairs)),
            sems((ITERS, pairs)),
            sems((ITERS, 2, pairs if groups > 1 else 1)),
            sems((ITERS, 2, MAXSHIFT if groups > 1 else 1)),
            *[pltpu.VMEM((pairs + 2 * MAXSHIFT,) + block, F32) for _ in range(ITERS)],
        ],
        compiler_params=pltpu.CompilerParams(
            collective_id=0, has_side_effects=True, vmem_limit_bytes=48 * 1024 * 1024
        ),
        cost_estimate=pl.CostEstimate(
            flops=flops, bytes_accessed=4 * retarded.size * 4, transcendentals=0
        ),
    )(retarded[0], injection[0], coupling_matrices, phonon_weight, phonon_shift, slice_neighbour)
    return lesser[None], sigma[None]


def solution(mesh):
    inner = mesh.shape["inner"]
    devices = mesh.shape["egrp"] * inner
    spread = P(("egrp", "inner"), None, None, None, None)

    def run(retarded, *others):
        pairs = retarded.shape[1] * retarded.shape[2]
        groups = devices // pairs
        assert retarded.shape[0] == devices and devices == groups * pairs
        return jax.shard_map(
            functools.partial(local, groups, inner),
            mesh=mesh,
            in_specs=(spread, spread, P(), P(), P(), P()),
            out_specs=(spread, spread),
            check_vma=False,
        )(retarded, *others)

    return run
```

time: 497 us -> 218 us (0.44); the launches traced: 488 us -> 214 us
  waiting for transfers between devices: 295 us -> 0 us
  Pallas kernels: 0 us -> 208 us
  starting transfers between devices: 77.1 us -> 0 us
  matrix products: 69.8 us -> 0 us
  other arithmetic: 21.9 us -> 0 us
  local copies, waits for them, and re-layouts: 18.5 us -> 5.53 us
  between operations: 6.26 us -> 0.65 us
    pallas_call x0 -> x1, Pallas kernels: none -> 208 us  [local(): pl.pallas_call(functools.partial(kernel, groups, inner, pairs), out_shape...]
    ppermute x8 -> x0, waiting for transfers between devices: 154 us -> none  [the longest x4 107 us: padded(): lax.ppermute(lax.slice_in_dim(block, 0, width, axis=dim), axis, backward)]
    all_to_all x4 -> x0, waiting for transfers between devices: 141 us -> none  [the longest x1 47.7 us: local(): lax.all_to_all(phonon_sigma, 'inner', split_axis=0, concat_axis=2, tiled=...]
    dot_general x26 -> x0, matrix products: 69.8 us -> none  [the longest x8 17 us: product_adjoint(): return jnp.einsum('...ij,...kj->...ik', first, second, precision=HIGHEST)]
    all_to_all x4 -> x0, starting transfers between devices: 48.1 us -> none  [the longest x1 24 us: local(): lax.all_to_all(phonon_sigma, 'inner', split_axis=0, concat_axis=2, tiled=...]
    ppermute x8 -> x0, starting transfers between devices: 29 us -> none  [the longest x4 23.4 us: padded(): lax.ppermute(lax.slice_in_dim(block, block.shape[dim] - width, None, axis...]
    add x5 -> x0, other arithmetic: 11 us -> none  [the longest x2 7.44 us: couple_block(): phonon_weight[phonon, 0] * shifted_up]
    concatenate x4 -> x0, other arithmetic: 9.09 us -> none  [padded(): block = jnp.concatenate([low, block, high], axis=dim)]
  transfers between devices with their start and end apart: 12 -> 0, of which waited for: 10 -> 0; matrix products, arithmetic and copies ran while one was open for 6% -> 0% of each run, Pallas kernels for 0% -> 0%
where the time goes in v1:
time: 218 us; the launch traced here: 214 us
  Pallas kernels  208 us (95%)
  local copies, waits for them, and re-layouts  5.53 us (3%)
    pallas_call x1, Pallas kernels, local(): pl.pallas_call(functools.partial(kernel, groups, inner, pairs), out_shape...  208 us
    unnamed x10, local copies, waits for them, and re-layouts  5.53 us

profile of v1, /device:TPU:0, one launch (start us, length us, event | category | flops | bytes accessed | tf_op | source)
XLA Modules:
  0.0 214.0 jit_solution(16003257621991964730)
XLA Ops:
  0.6 0.0 copy-start
  0.6 0.9 copy-done
  1.5 0.0 copy-start.1
  1.5 0.7 copy-done.1
  2.2 0.0 copy-start.2
  2.2 0.7 copy-done.2
  2.9 0.0 copy-start.3
  2.9 0.7 copy-done.3
  3.5 207.9 %shard_map.77 = (f32[2,16,128,128]{3,2,1,0:T(8,128)S(1)}, f32[2,16,128,128]{3,2,1,0:T(8,128)S(1)}) custom-call(f32[2,16,128,128]{3,2,1,0:T(8,128)} %bitcast.6, f32[2,16,128,128]{3,2,1,0:T(8,128)} %bitcast.7, f32[2,128,128]{2,1,0:T(8,128)S(1)} %copy-done, f32[2,2]{1,0:T(2,128)S(1)} %copy-done.1, s32[2]{0:T(128)S(1)} %copy-done.2, s32[16]{0:T(128)S(1)} %copy-done.3), custom_call_target="tpu_custom_call" | custom-call | flops 6442450944 | bytes 8388608 | tf_op jit(solution)/shard_map/pallas_call | solution.py:273
  211.4 1.3 copy.10
  212.7 1.3 copy.11
Async XLA Ops:
  0.6 0.9 copy-start
  1.5 0.7 copy-start.1
  2.2 0.7 copy-start.2
  2.9 0.7 copy-start.3

commit v2 on v1

--- a/solution.py
+++ b/solution.py
@@ -39,7 +39,7 @@
     groups, inner, pairs,
     ret_ref, inj_ref, coupling_ref, weight_ref, shift_ref, near_ref,
     lesser_ref, sigma_ref,
-    mix_buf, k_buf, sig_buf,
+    mix_buf, k_buf, sig_buf, z_buf,
     mix_send, mix_recv, sig_send, sig_recv, halo_send, halo_recv,
     *x_bufs,
 ):
@@ -72,15 +72,10 @@
 
                 lax.fori_loop(0, pairs, greet_side, 0)
 
-    zeros = jnp.zeros((MAXSHIFT,) + x_bufs[0].shape[1:], F32)
-    for iteration in range(ITERS):
-        @pl.when(group == 0)
-        def _():
-            x_bufs[iteration][pl.ds(0, MAXSHIFT)] = zeros
-
-        @pl.when(group == groups - 1)
-        def _():
-            x_bufs[iteration][pl.ds(MAXSHIFT + pairs, MAXSHIFT)] = zeros
+    zeros = jnp.zeros((MAXSHIFT,) + z_buf.shape[2:], F32)
+    for m in range(z_buf.shape[0]):
+        z_buf[m, pl.ds(0, MAXSHIFT)] = zeros
+        z_buf[m, pl.ds(MAXSHIFT + pairs, MAXSHIFT)] = zeros
 
     def sandwich(iteration, s):
         source_real, source_imag = inj_ref[0, s], inj_ref[1, s]
@@ -160,41 +155,49 @@
             device_id_type=MESH,
         )
 
-    coupling = [halves(coupling_ref[m]) for m in range(coupling_ref.shape[0])]
-    wide = [jnp.concatenate(list(part), axis=1) for part in zip(*coupling)]
-
-    def couple(iteration, energy):
-        halfway = []
-        for m in range(len(coupling)):
+    modes = coupling_ref.shape[0]
+    size = coupling_ref.shape[1]
+    coupling = [halves(coupling_ref[m]) for m in range(modes)]
+    tall = [jnp.concatenate(list(part), axis=0) for part in zip(*coupling)]
+
+    def project(iteration, slots):
+        blocks = [halves(x_bufs[iteration][slot]) for slot in slots]
+        side = [jnp.concatenate(list(part), axis=1) for part in zip(*blocks)]
+        halfway = halves(dot3(tall, side, PLAIN))
+        for m in range(modes):
+            rows = slice(m * size, (m + 1) * size)
+            stacked = [
+                jnp.concatenate(
+                    [part[rows, i * size:(i + 1) * size] for i in range(len(slots))], axis=0
+                )
+                for part in halfway
+            ]
+            done = dot3(stacked, coupling[m], ADJOINT)
+            for i, slot in enumerate(slots):
+                z_buf[m, slot] = done[i * size:(i + 1) * size]
+
+    def couple(energy):
+        total = None
+        for m in range(modes):
             shift = shift_ref[m]
-            summed = (
-                weight_ref[m, 0] * x_bufs[iteration][MAXSHIFT + energy + shift]
-                + weight_ref[m, 1] * x_bufs[iteration][MAXSHIFT + energy - shift]
+            term = (
+                weight_ref[m, 0] * z_buf[m, MAXSHIFT + energy + shift]
+                + weight_ref[m, 1] * z_buf[m, MAXSHIFT + energy - shift]
             )
-            halfway.append(halves(dot3(coupling[m], halves(summed), PLAIN)))
-        joined = [jnp.concatenate(list(part), axis=1) for part in zip(*halfway)]
-        return dot3(joined, wide, ADJOINT)
+            total = term if total is None else total + term
+        return total
 
     for iteration in range(ITERS):
-        def do_sandwich(s, carry):
-            sandwich(iteration, s)
-            return carry
-
-        lax.fori_loop(0, slices, do_sandwich, 0)
-
-        if iteration == 0:
-            if groups > 1:
-                sides = (group > 0).astype(jnp.int32) + (group < groups - 1).astype(jnp.int32)
-                pl.semaphore_wait(barrier, pairs - 1 + sides * pairs)
-            else:
-                pl.semaphore_wait(barrier, pairs - 1)
+        way = 1 if iteration % 2 == 0 else -1
+
+        def slice_at(step):
+            return (my_slice + way * step + slices) % slices
 
         def mixed(pair):
             part, s = pair % 2, pair // 2
             return lesser_ref[part, s] + 0.5 * lesser_ref[part, near_ref[s]]
 
-        def do_mix(step, carry):
-            pair = (mine + step) % pairs
+        def send_mixed(pair):
             mix_buf[iteration, pair] = mixed(pair)
             mix_copy(iteration, pair, mine).start()
             if groups > 1:
@@ -202,9 +205,36 @@
                     @pl.when(sends_halo(side))
                     def _():
                         halo_copy(iteration, side, pair).start()
+
+        def do_sandwich(step, carry):
+            s = slice_at(step)
+            if iteration > 0:
+                for part in range(2):
+                    sigma_copy(iteration - 1, mine, 2 * s + part).wait_recv()
+            sandwich(iteration, s)
             return carry
 
-        lax.fori_loop(1, pairs, do_mix, 0)
+        def do_slice(step, carry):
+            do_sandwich(step, carry)
+            s = slice_at(step - 1)
+            for part in range(2):
+                send_mixed(2 * s + part)
+            return carry
+
+        if iteration > 0:
+            sigma_copy(iteration - 1, mine, 2 * my_slice + 1 - my_part).wait_recv()
+        sandwich(iteration, my_slice)
+        do_sandwich(1, 0)
+        if iteration == 0:
+            if groups > 1:
+                sides = (group > 0).astype(jnp.int32) + (group < groups - 1).astype(jnp.int32)
+                pl.semaphore_wait(barrier, pairs - 1 + sides * pairs)
+            else:
+                pl.semaphore_wait(barrier, pairs - 1)
+        lax.fori_loop(2, slices, do_slice, 0)
+        for part in range(2):
+            send_mixed(2 * slice_at(slices - 1) + part)
+        send_mixed(2 * my_slice + 1 - my_part)
         own = mixed(mine)
         x_bufs[iteration][MAXSHIFT + mine] = own
         if groups > 1:
@@ -214,33 +244,48 @@
                 def _():
                     halo_copy(iteration, side, mine).start()
 
-        def mix_arrives(step, carry):
-            mix_copy(iteration, mine, (mine + pairs - step) % pairs).wait_recv()
+        def source_at(step):
+            return (mine - way * step + pairs) % pairs
+
+        def arrival(step):
+            mix_copy(iteration, mine, source_at(step)).wait_recv()
+
+        def project_at(step):
+            project(iteration, [MAXSHIFT + source_at(step), MAXSHIFT + source_at(step + 1)])
+
+        def do_project(step, carry):
+            arrival(2 * step)
+            arrival(2 * step + 1)
+            project_at(2 * step)
             return carry
 
-        lax.fori_loop(1, pairs, mix_arrives, 0)
+        arrival(1)
+        project_at(0)
+        lax.fori_loop(1, slices, do_project, 0)
         if groups > 1:
             for side in (0, 1):
                 @pl.when(gets_halo(side))
                 def _():
+                    start = MAXSHIFT + pairs if side == 0 else 0
                     for slot in range(MAXSHIFT):
                         halo_arrival(iteration, side, slot).wait_recv()
+                        project(iteration, [start + slot])
 
         def do_couple(step, carry):
             energy = (mine + step) % pairs
-            k_buf[iteration, energy] = couple(iteration, energy)
+            k_buf[iteration, energy] = couple(energy)
             sigma_copy(iteration, energy, mine).start()
             return carry
 
         lax.fori_loop(1, pairs, do_couple, 0)
         target = sig_buf if iteration + 1 < ITERS else sigma_ref
-        target[my_part, my_slice] = couple(iteration, mine)
-
-        def sigma_arrives(step, carry):
-            sigma_copy(iteration, mine, (mine + pairs - step) % pairs).wait_recv()
-            return carry
-
-        lax.fori_loop(1, pairs, sigma_arrives, 0)
+        target[my_part, my_slice] = couple(mine)
+
+    def sigma_arrives(step, carry):
+        sigma_copy(ITERS - 1, mine, (mine + pairs - step) % pairs).wait_recv()
+        return carry
+
+    lax.fori_loop(1, pairs, sigma_arrives, 0)
 
     def drain(step, carry):
         other = (mine + step) % pairs
@@ -266,6 +311,7 @@
     shape = retarded.shape[1:]
     block = shape[2:]
     pairs = shape[0] * shape[1]
+    modes = coupling_matrices.shape[0]
     vmem = pl.BlockSpec(memory_space=pltpu.VMEM)
     smem = pl.BlockSpec(memory_space=pltpu.SMEM)
     sems = pltpu.SemaphoreType.DMA
@@ -279,6 +325,7 @@
             pltpu.VMEM((ITERS, pairs) + block, F32),
             pltpu.VMEM((ITERS, pairs) + block, F32),
             pltpu.VMEM(shape, F32),
+            pltpu.VMEM((modes, pairs + 2 * MAXSHIFT) + block, F32),
             sems((ITERS, pairs)),
             sems((ITERS, pairs)),
             sems((ITERS, pairs)),

time: 218 us -> 205 us (0.940)
  Pallas kernels: 208 us -> 196 us
    pallas_call x1, Pallas kernels: 208 us -> 196 us  [local(): pl.pallas_call(functools.partial(kernel, groups, inner, pairs), out_shape...]
where the time goes in v2:
time: 205 us; the launch traced here: 202 us
  Pallas kernels  196 us (96%)
  local copies, waits for them, and re-layouts  5.53 us (3%)
    pallas_call x1, Pallas kernels, local(): pl.pallas_call(functools.partial(kernel, groups, inner, pairs), out_shape...  196 us
    unnamed x10, local copies, waits for them, and re-layouts  5.53 us

profile of v2, /device:TPU:0, one launch (start us, length us, event | category | flops | bytes accessed | tf_op | source)
XLA Modules:
  0.0 202.3 jit_solution(4818370762229976030)
XLA Ops:
  0.6 0.0 copy-start
  0.6 0.9 copy-done
  1.5 0.0 copy-start.1
  1.5 0.7 copy-done.1
  2.2 0.0 copy-start.2
  2.2 0.7 copy-done.2
  2.9 0.0 copy-start.3
  2.9 0.7 copy-done.3
  3.5 196.1 %shard_map.77 = (f32[2,16,128,128]{3,2,1,0:T(8,128)S(1)}, f32[2,16,128,128]{3,2,1,0:T(8,128)S(1)}) custom-call(f32[2,16,128,128]{3,2,1,0:T(8,128)} %bitcast.6, f32[2,16,128,128]{3,2,1,0:T(8,128)} %bitcast.7, f32[2,128,128]{2,1,0:T(8,128)S(1)} %copy-done, f32[2,2]{1,0:T(2,128)S(1)} %copy-done.1, s32[2]{0:T(128)S(1)} %copy-done.2, s32[16]{0:T(128)S(1)} %copy-done.3), custom_call_target="tpu_custom_call" | custom-call | flops 6442450944 | bytes 8388608 | tf_op jit(solution)/shard_map/pallas_call | solution.py:319
  199.7 1.3 copy.10
  201.0 1.3 copy.11
Async XLA Ops:
  0.6 0.9 copy-start
  1.5 0.7 copy-start.1
  2.2 0.7 copy-start.2
  2.9 0.7 copy-start.3
